TPU v7x, 512 devices: a whole 4x8x8 slice. The times are simulated.
512 devices in a mesh: resp: 16 (over y_hi, x), head: 4 (over y_lo, core), grp: 8 (over z).
Axes of the slice: x: 4, y: 8 (y_hi: 4, y_lo: 2; y = y_hi * 2 + y_lo), z: 8, core: 2. Of those that a mesh axis runs over, the one named last changes fastest.
Arguments:
- q_prompt: bfloat16 [8, 1024, 32, 128], P('grp', 'resp', 'head'), may hold values from -6 to 6
- q_resp: bfloat16 [8, 16, 128, 32, 128], P('grp', 'resp', None, 'head'), may hold values from -6 to 6
- kv_prompt: bfloat16 [8, 2, 1024, 4, 128], P('grp', None, 'resp', 'head'), may hold values from -6 to 6
- kv_resp: bfloat16 [8, 16, 2, 128, 4, 128], P('grp', 'resp', None, None, 'head'), may hold values from -6 to 6
- dout_prompt: bfloat16 [8, 1024, 32, 128], P('grp', 'resp', 'head'), may hold values from -21 to 21
- dout_resp: bfloat16 [8, 16, 128, 32, 128], P('grp', 'resp', None, 'head'), may hold values from -21 to 21
- q_gain: float32 [128], replicated, may hold values from 0.1 to 1.9
- k_gain: float32 [128], replicated, may hold values from 0.1 to 1.9
- resp_len: int32 [8, 16], P('grp', 'resp'), may hold values from 16 to 128, as said below
- prompt_len: int32 [8], P('grp'), may hold values from 512 to 1024, as said below
Outputs:
- dq_prompt: bfloat16 [8, 1024, 32, 128], P('grp', 'resp', 'head')
- dq_resp: bfloat16 [8, 16, 128, 32, 128], P('grp', 'resp', None, 'head')
- dkv_prompt: bfloat16 [8, 2, 1024, 4, 128], P('grp', None, 'resp', 'head')
- dkv_resp: bfloat16 [8, 16, 2, 128, 4, 128], P('grp', 'resp', None, None, 'head')
- gain_grads: float32 [2, 128], replicated
Inputs may be any that keep to these rules, and one draw needn't show every extreme that they name: `resp_len`: in every group some response uses all 128 positions. `prompt_len`: some group uses all 1024 prompt positions.
All inputs are finite; a program needn't handle non-finite values.
Results may differ from a plain program's by a relative error of at most 0.0098.
Values may be sent and summed in bfloat16 or wider, within the bound.
A program may use at most 64 MiB of HBM per device.

v0:
```python
import functools
import math

import jax
import jax.numpy as jnp
from jax import lax
from jax.experimental import pallas as pl
from jax.experimental.pallas import tpu as pltpu
from jax.sharding import PartitionSpec as P

EPSILON = 1e-06
MESH = pl.DeviceIdType.MESH
HD = 128
BF = jnp.bfloat16
F32 = jnp.float32
NX = 4
NY = 4
TILE = 512
FARTHEST_FIRST = (4, 3, 5, 2, 6, 1, 7)
NT = (((1,), (1,)), ((), ()))
NN = (((1,), (0,)), ((), ()))


def dot(lhs, rhs, dims=NN):
    return lax.dot_general(lhs, rhs, dims, preferred_element_type=F32)


def order(step):
    return step + step // 2 - 2 * (step // 3)


def kernel(
    qr_in,
    qp_in,
    kvp_in,
    kvr_in,
    dr_in,
    dp_in,
    qg_in,
    kg_in,
    rlen_in,
    plen_in,
    dqr_out,
    dqp_out,
    dkvp_out,
    dkvr_out,
    gains_out,
    qg_ref,
    kg_ref,
    rlen_ref,
    plen_ref,
    q_nat,
    d_nat,
    kvr,
    kall,
    unit_qt,
    inv_q,
    qnt,
    qn,
    dt,
    dst,
    delta_ref,
    gcol,
    kn_ref,
    knt_ref,
    vt1,
    knr,
    knrt,
    ukr,
    e_ref,
    er_ref,
    gs_ref,
    gsr_ref,
    ol,
    sums,
    vsum,
    part,
    rx,
    own,
    ys,
    ry,
    kterm,
    gsend,
    grecv,
    dq_v,
    dkvp_v,
    dkvr_v,
    in_sem,
    out_sem,
    kvx_got,
    kvy_got,
    kv_sent,
    rx_got,
    rx_sent,
    ry_got,
    ry_sent,
    g_got,
    g_sent,
    z_ready,
):
    resp = lax.axis_index("resp")
    head = lax.axis_index("head")
    grp = lax.axis_index("grp")
    yh = resp // NX
    x = lax.rem(resp, NX)
    yl = head // 2
    core = lax.rem(head, 2)
    ngrp = 8
    y8 = 2 * yh + yl
    rows_r = qr_in.shape[0]
    rows_p = qp_in.shape[0]
    rows = rows_r + rows_p
    tiles = rows // TILE
    tiles_r = rows_r // TILE
    scale = HD**-0.5
    exp_scale = scale * math.log2(math.e)

    def partner(stage, k):
        if stage == 0:
            to = lax.rem(y8 + k, 8)
            return {"resp": (to // 2) * NX + x, "head": lax.rem(to, 2) * 2 + core}
        if stage == 1:
            to = lax.rem(2 * x + core + k, 8)
            return {"resp": yh * NX + to // 2, "head": yl * 2 + lax.rem(to, 2)}
        return {"grp": lax.rem(grp + k, ngrp)}

    stage_at = (y8, 2 * x + core, grp)

    loads = [
        pltpu.make_async_copy(kvp_in, kall.at[resp], in_sem.at[0]),
        pltpu.make_async_copy(qr_in, q_nat.at[pl.ds(0, rows_r)], in_sem.at[1]),
        pltpu.make_async_copy(qp_in, q_nat.at[pl.ds(rows_r, rows_p)], in_sem.at[2]),
        pltpu.make_async_copy(kvr_in, kvr, in_sem.at[3]),
        pltpu.make_async_copy(dr_in, d_nat.at[pl.ds(0, rows_r)], in_sem.at[4]),
        pltpu.make_async_copy(dp_in, d_nat.at[pl.ds(rows_r, rows_p)], in_sem.at[5]),
        pltpu.make_async_copy(qg_in, qg_ref, in_sem.at[6]),
        pltpu.make_async_copy(kg_in, kg_ref, in_sem.at[7]),
        pltpu.make_async_copy(rlen_in, rlen_ref, in_sem.at[8]),
        pltpu.make_async_copy(plen_in, plen_ref, in_sem.at[9]),
    ]
    loads[0].start()
    barrier = pltpu.get_barrier_semaphore()
    for k in FARTHEST_FIRST:
        for stage in (0, 1):
            pl.semaphore_signal(
                barrier, inc=1, device_id=partner(stage, k), device_id_type=MESH
            )
    for k in range(7, 0, -1):

        @pl.when(grp + k < ngrp)
        def _(k=k):
            pl.semaphore_signal(
                barrier, inc=1, device_id={"grp": grp + k}, device_id_type=MESH
            )

    loads[0].wait()
    pl.semaphore_wait(barrier, 14 + grp)

    def remote(src, dst, sent, got, to):
        return pltpu.make_async_remote_copy(
            src_ref=src,
            dst_ref=dst,
            send_sem=sent,
            recv_sem=got,
            device_id={"resp": to},
            device_id_type=MESH,
        )

    def wait_for(ref, sem):
        pltpu.make_async_copy(ref, ref, sem).wait()

    def x_peer(dx):
        return yh * NX + lax.rem(x + dx, NX)

    def y_peer(dy):
        return lax.rem(yh + dy, NY) * NX + x

    def chunk_at(slot):
        return lax.rem(yh + order(slot), NY)

    def along_x(slot):
        block = kall.at[chunk_at(slot) * NX + x]
        for dx in (2, 1, 3):
            remote(block, block, kv_sent, kvx_got.at[slot], x_peer(dx)).start()

    for dy in (2, 1, 3):
        remote(
            kall.at[resp], kall.at[resp], kv_sent, kvy_got.at[dy - 1], y_peer(dy)
        ).start()
    along_x(0)
    for load in loads[1:]:
        load.start()

    def forward(slot):
        dy = (0, 1, 3, 2)[slot]
        wait_for(kall.at[y_peer(dy)], kvy_got.at[(4 - dy) - 1])
        along_x(slot)

    for load in loads[6:]:
        load.wait()
    plen = plen_ref[0]
    rlen = rlen_ref[0, 0]

    gcol[...] = jnp.broadcast_to(qg_ref[...], (TILE, HD)).T
    loads[1].wait()
    loads[2].wait()
    for n in range(tiles):
        sl = pl.ds(n * TILE, TILE)
        xt = q_nat[sl, :].T.astype(F32)
        inv = lax.rsqrt(jnp.mean(xt * xt, axis=0, keepdims=True) + EPSILON)
        ut = xt * inv
        unit_qt[:, sl] = ut
        inv_q[:, sl] = jnp.broadcast_to(inv, (8, TILE))
        qt = (ut * gcol[...]).astype(BF)
        qnt[:, sl] = qt
        qn[sl, :] = qt.T

    forward(1)
    forward(2)
    for k in range(7, 0, -1):

        @pl.when(grp >= k)
        def _(k=k):
            pl.semaphore_signal(
                z_ready, inc=1, device_id={"grp": grp - k}, device_id_type=MESH
            )


    loads[4].wait()
    loads[5].wait()
    for n in range(tiles):
        sl = pl.ds(n * TILE, TILE)
        lane = lax.broadcasted_iota(jnp.int32, (HD, TILE), 1) + n * TILE
        if n < tiles_r:
            keep = lane < rlen * 8
        else:
            keep = lane - rows_r < (plen - rows_p // 8 * resp) * 8
        dt[:, sl] = jnp.where(keep, d_nat[sl, :].T.astype(F32), 0.0)

    loads[3].wait()
    kf = kvr[0].astype(F32)
    inv_kr = lax.rsqrt(jnp.mean(kf * kf, axis=-1, keepdims=True) + EPSILON)
    ur = kf * inv_kr
    ukr[...] = ur
    kr = (ur * kg_ref[...]).astype(BF)
    knr[...] = kr
    knrt[...] = kr.T
    nkr = kr.shape[0]
    vt1[pl.ds(0, HD), pl.ds(0, nkr)] = kvr[1].T
    vt1[pl.ds(HD, 16), pl.ds(0, nkr)] = jnp.ones((16, nkr), BF)
    for n in range(tiles):
        sl = pl.ds(n * TILE, TILE)
        if n < tiles_r:
            s = dot(knr[...], qnt[:, sl])
            at = lax.broadcasted_iota(jnp.int32, s.shape, 0)
            lane = lax.broadcasted_iota(jnp.int32, s.shape, 1) + n * TILE
            e = jnp.where(at * 8 <= lane, jnp.exp2(s * exp_scale), 0.0).astype(BF)
            er_ref[:, sl] = e
            ol[:, sl] = dot(vt1[:, pl.ds(0, nkr)], e)
        else:
            ol[:, sl] = jnp.zeros((HD + 16, TILE), F32)

    forward(3)

    def pass1(step, carry):
        chunk = chunk_at(step)
        wait_for(kall.at[pl.ds(0, NX - 1)], kvx_got.at[step])
        n_keys = NX * kall.shape[2]
        at = lax.broadcasted_iota(jnp.int32, (n_keys, HD), 0) + chunk * n_keys
        k_raw = kall[pl.ds(chunk * NX, NX), 0].reshape(n_keys, HD).astype(F32)
        inv = lax.rsqrt(jnp.mean(k_raw * k_raw, axis=-1, keepdims=True) + EPSILON)
        unit = k_raw * inv
        kf = unit * kg_ref[...]
        kn = kf.astype(BF)
        kn_ref[step] = kn
        knt_ref[step] = jnp.where(at < plen, kf, 0.0).astype(BF).T
        v = kall[pl.ds(chunk * NX, NX), 1].reshape(n_keys, HD).astype(F32)
        vt1[pl.ds(0, HD), :] = jnp.where(at < plen, v, 0.0).astype(BF).T
        lane = lax.broadcasted_iota(jnp.int32, (16, n_keys), 1) + chunk * n_keys
        vt1[pl.ds(HD, 16), :] = jnp.where(lane < plen, 1.0, 0.0).astype(BF)
        ahead_s = dot(kn, qnt[:, pl.ds(0, TILE)])
        for n in range(tiles):
            sl = pl.ds(n * TILE, TILE)
            s = ahead_s
            if n + 1 < tiles:
                ahead_s = dot(kn, qnt[:, pl.ds((n + 1) * TILE, TILE)])
            e = jnp.exp2(s * exp_scale)
            if n >= tiles_r:
                key = lax.broadcasted_iota(jnp.int32, s.shape, 0)
                lane = lax.broadcasted_iota(jnp.int32, s.shape, 1) + (n * TILE - rows_r)
                ahead = resp * (rows_p // 8) - chunk * n_keys
                e = jnp.where((key - ahead) * 8 <= lane, e, 0.0)
            e = e.astype(BF)
            e_ref[step, :, sl] = e
            ol[:, sl] += dot(vt1[...], e)
        return carry

    lax.fori_loop(0, NY, pass1, 0)

    for n in range(tiles):
        sl = pl.ds(n * TILE, TILE)
        rl = 1.0 / ol[pl.ds(HD, 1), sl]
        ds = (dt[:, sl] * rl).astype(BF)
        dst[:, sl] = ds
        delta = rl * jnp.sum(ds.astype(F32) * ol[pl.ds(0, HD), sl], axis=0, keepdims=True)
        delta_ref[:, sl] = jnp.broadcast_to(delta, (8, TILE))
    kterm[...] = jnp.zeros((8, HD), F32)

    def summed(slot, which):
        total = own[slot, which]
        for k in range(NX - 1):
            total = total + rx[slot, k, which].astype(F32)
        return total

    def along_y(slot):
        dy = (0, 1, 3, 2)[slot]
        wait_for(rx.at[slot], rx_got.at[slot])
        for which in range(2):
            ys[slot, which] = summed(slot, which).astype(BF)
        remote(ys.at[slot], ry.at[dy - 1], ry_sent, ry_got, y_peer(dy)).start()

    span = kall.shape[2]

    def pass2(back, carry):
        step = NY - 1 - back
        chunk = chunk_at(step)
        n_keys = NX * span
        v = kall[pl.ds(chunk * NX, NX), 1].reshape(n_keys, HD)
        gk = jnp.zeros((n_keys, HD), F32)
        ahead_dp = dot(v, dst[:, pl.ds(0, TILE)])
        for n in range(tiles):
            sl = pl.ds(n * TILE, TILE)
            dp = ahead_dp
            if n + 1 < tiles:
                ahead_dp = dot(v, dst[:, pl.ds((n + 1) * TILE, TILE)])
            e = e_ref[step, :, sl].astype(F32)
            gs = (e * (dp - delta_ref[pl.ds(0, 1), sl])).astype(BF)
            gs_ref[step, :, sl] = gs
            gk += dot(gs, qn[sl, :])
        at = lax.broadcasted_iota(jnp.int32, (n_keys, HD), 0) + chunk * n_keys
        gk = jnp.where(at < plen, gk * scale, 0.0)
        kn = kn_ref[step].astype(F32)
        kterm[...] += jnp.sum((gk * kn).reshape(n_keys // 8, 8, HD), axis=0)
        sums[step] = gk
        return carry

    lax.fori_loop(0, NY, pass2, 0)

    gkr = jnp.zeros((nkr, HD), F32)
    for n in range(tiles_r):
        sl = pl.ds(n * TILE, TILE)
        dp = dot(kvr[1], dst[:, sl])
        e = er_ref[:, sl].astype(F32)
        gs = (e * (dp - delta_ref[pl.ds(0, 1), sl])).astype(BF)
        gsr_ref[:, sl] = gs
        gkr += dot(gs, qn[sl, :])
    gkr = gkr * scale
    kn = knr[...].astype(F32)
    kterm[...] += jnp.sum((gkr * kn).reshape(nkr // 8, 8, HD), axis=0)

    stores = [
        pltpu.make_async_copy(dkvr_v, dkvr_out, out_sem.at[0]),
        pltpu.make_async_copy(dq_v.at[pl.ds(0, rows_r)], dqr_out, out_sem.at[1]),
        pltpu.make_async_copy(dq_v.at[pl.ds(rows_r, rows_p)], dqp_out, out_sem.at[2]),
        pltpu.make_async_copy(dkvp_v, dkvp_out, out_sem.at[3]),
        pltpu.make_async_copy(gsend.at[3, pl.ds(0, 2)], gains_out, out_sem.at[4]),
    ]
    term = jnp.sum(kterm[...], axis=0, keepdims=True)
    qterm = term / qg_ref[...]
    key_sum = term / kg_ref[...]
    which_row = lax.broadcasted_iota(jnp.int32, (8, HD), 0)
    gsend[0] = jnp.where(
        which_row == 0,
        jnp.broadcast_to(qterm, (8, HD)),
        jnp.where(which_row == 1, jnp.broadcast_to(key_sum, (8, HD)), 0.0),
    )

    def g_start(stage):
        for k in FARTHEST_FIRST:
            pltpu.make_async_remote_copy(
                src_ref=gsend.at[stage],
                dst_ref=grecv.at[stage, stage_at[stage]],
                send_sem=g_sent,
                recv_sem=g_got.at[stage],
                device_id=partner(stage, k),
                device_id_type=MESH,
            ).start()
        grecv[stage, stage_at[stage]] = gsend[stage]

    def g_finish(stage):
        wait_for(grecv.at[stage, pl.ds(0, 7)], g_got.at[stage])
        total = grecv[stage, 0]
        for k in range(1, 8):
            total = total + grecv[stage, k]
        gsend[stage + 1] = total

    g_start(0)

    def pass3(back, carry):
        step = NY - 1 - back
        n_keys = NX * span
        at = lax.broadcasted_iota(jnp.int32, (n_keys, HD), 0) + chunk_at(step) * n_keys
        gv = dot(e_ref[step], dst[...], NT)
        vsum[...] = jnp.where(at < plen, gv, 0.0)
        for k in range(NX):
            part[step, k, 0] = sums[step, pl.ds(k * span, span), :].astype(BF)
            part[step, k, 1] = vsum[pl.ds(k * span, span), :].astype(BF)
        own[step, 0] = sums[step, pl.ds(x * span, span), :]
        own[step, 1] = vsum[pl.ds(x * span, span), :]
        for dx in (2, 1, 3):
            remote(
                part.at[step, lax.rem(x + dx, NX)],
                rx.at[step, dx - 1],
                rx_sent,
                rx_got.at[step],
                x_peer(dx),
            ).start()
        return carry

    lax.fori_loop(0, NY, pass3, 0)

    g_finish(0)
    g_start(1)

    gvr = dot(er_ref[...], dst[:, pl.ds(0, rows_r)], NT)
    ur = ukr[...]
    kf = kvr[0].astype(F32)
    inv = lax.rsqrt(jnp.mean(kf * kf, axis=-1, keepdims=True) + EPSILON)
    gu = gkr * kg_ref[...]
    dk = inv * (gu - ur * jnp.mean(gu * ur, axis=-1, keepdims=True))
    dkvr_v[0] = dk.astype(BF)
    dkvr_v[1] = gvr.astype(BF)
    stores[0].start()


    for n in range(tiles):
        sl = pl.ds(n * TILE, TILE)
        gq = dot(knt_ref[0], gs_ref[0, :, sl])
        for slot in range(1, NY):
            gq += dot(knt_ref[slot], gs_ref[slot, :, sl])
        if n < tiles_r:
            gq += dot(knrt[...], gsr_ref[:, sl])
        ut = unit_qt[:, sl]
        gu = gq * scale * gcol[...]
        back = inv_q[pl.ds(0, 1), sl] * (gu - ut * jnp.mean(gu * ut, axis=0, keepdims=True))
        dq_v[sl, :] = back.astype(BF).T
    stores[1].start()
    stores[2].start()

    g_finish(1)

    @pl.when(grp < ngrp - 1)
    def _():
        pl.semaphore_wait(z_ready, ngrp - 1 - grp)

    g_start(2)
    for slot in (3, 2, 1):
        along_y(slot)
    wait_for(rx.at[0], rx_got.at[0])
    totals = [summed(0, which) for which in range(2)]
    kf = kall[resp, 0].astype(F32)
    inv = lax.rsqrt(jnp.mean(kf * kf, axis=-1, keepdims=True) + EPSILON)
    unit = kf * inv
    wait_for(kall.at[pl.ds(0, 15)], kv_sent)
    wait_for(rx, rx_sent)

    wait_for(ry, ry_got)
    for which in range(2):
        for k in range(NY - 1):
            totals[which] = totals[which] + ry[k, which].astype(F32)
    gu = totals[0] * kg_ref[...]
    dk = inv * (gu - unit * jnp.mean(gu * unit, axis=-1, keepdims=True))
    dkvp_v[0] = dk.astype(BF)
    dkvp_v[1] = totals[1].astype(BF)
    stores[3].start()
    wait_for(ry, ry_sent)

    g_finish(2)
    stores[4].start()
    wait_for(grecv.at[:, pl.ds(0, 7)], g_sent)
    for store in stores:
        store.wait()


def hand_out(*refs):
    ins, outs, held = refs[:5], refs[5:10], refs[10:15]
    in_sem, out_sem = refs[15:]
    loads = [pltpu.make_async_copy(ins[n], held[n], in_sem.at[n]) for n in range(5)]
    stores = [pltpu.make_async_copy(held[n], outs[n], out_sem.at[n]) for n in range(5)]
    for load in loads:
        load.start()
    for load, store in zip(loads, stores):
        load.wait()
        store.start()
    for store in stores:
        store.wait()


def shards(
    q_prompt,
    q_resp,
    kv_prompt,
    kv_resp,
    dout_prompt,
    dout_resp,
    q_gain,
    k_gain,
    resp_len,
    prompt_len,
):
    span = q_prompt.shape[1]
    length = q_resp.shape[2]
    rows_r = length * 8
    rows_p = span * 8
    rows = rows_r + rows_p
    n_keys = NX * span
    any_spec = pl.BlockSpec(memory_space=pl.ANY)
    hbm = pl.BlockSpec(memory_space=pltpu.HBM)
    dma = pltpu.SemaphoreType.DMA
    out = pl.pallas_call(
        kernel,
        out_shape=(
            jax.ShapeDtypeStruct((rows_r, HD), BF),
            jax.ShapeDtypeStruct((rows_p, HD), BF),
            jax.ShapeDtypeStruct((2, span, HD), BF),
            jax.ShapeDtypeStruct((2, length, HD), BF),
            jax.ShapeDtypeStruct((2, HD), F32),
        ),
        in_specs=[hbm] * 10,
        out_specs=[any_spec] * 5,
        scratch_shapes=[
            pltpu.VMEM((1, HD), F32),
            pltpu.VMEM((1, HD), F32),
            pltpu.SMEM((1, 1), jnp.int32),
            pltpu.SMEM((1,), jnp.int32),
            pltpu.VMEM((rows, HD), BF),
            pltpu.VMEM((rows, HD), BF),
            pltpu.VMEM((2, length, HD), BF),
            pltpu.VMEM((NX * NY, 2, span, HD), BF),
            pltpu.VMEM((HD, rows), F32),
            pltpu.VMEM((8, rows), F32),
            pltpu.VMEM((HD, rows), BF),
            pltpu.VMEM((rows, HD), BF),
            pltpu.VMEM((HD, rows), F32),
            pltpu.VMEM((HD, rows), BF),
            pltpu.VMEM((8, rows), F32),
            pltpu.VMEM((HD, TILE), F32),
            pltpu.VMEM((NY, n_keys, HD), BF),
            pltpu.VMEM((NY, HD, n_keys), BF),
            pltpu.VMEM((HD + 16, n_keys), BF),
            pltpu.VMEM((length, HD), BF),
            pltpu.VMEM((HD, length), BF),
            pltpu.VMEM((length, HD), F32),
            pltpu.VMEM((NY, n_keys, rows), BF),
            pltpu.VMEM((length, rows_r), BF),
            pltpu.VMEM((NY, n_keys, rows), BF),
            pltpu.VMEM((length, rows_r), BF),
            pltpu.VMEM((HD + 16, rows), F32),
            pltpu.VMEM((NY, n_keys, HD), F32),
            pltpu.VMEM((n_keys, HD), F32),
            pltpu.VMEM((NY, NX, 2, span, HD), BF),
            pltpu.VMEM((NY, NX - 1, 2, span, HD), BF),
            pltpu.VMEM((NY, 2, span, HD), F32),
            pltpu.VMEM((NY, 2, span, HD), BF),
            pltpu.VMEM((NY - 1, 2, span, HD), BF),
            pltpu.VMEM((8, HD), F32),
            pltpu.VMEM((4, 8, HD), F32),
            pltpu.VMEM((3, 8, 8, HD), F32),
            pltpu.VMEM((rows, HD), BF),
            pltpu.VMEM((2, span, HD), BF),
            pltpu.VMEM((2, length, HD), BF),
            dma((10,)),
            dma((5,)),
            dma((NY,)),
            dma((NY - 1,)),
            dma,
            dma((NY,)),
            dma,
            dma,
            dma,
            dma((3,)),
            dma,
            pltpu.SemaphoreType.REGULAR,
        ],
        compiler_params=pltpu.CompilerParams(
            collective_id=0, has_side_effects=True, vmem_limit_bytes=62 * 2**20
        ),
        name="attention_grads",
    )(
        q_resp.reshape(rows_r, HD),
        q_prompt.reshape(rows_p, HD),
        kv_prompt.reshape(2, span, HD),
        kv_resp.reshape(2, length, HD),
        dout_resp.reshape(rows_r, HD),
        dout_prompt.reshape(rows_p, HD),
        q_gain.reshape(1, HD),
        k_gain.reshape(1, HD),
        resp_len,
        prompt_len,
    )
    out = pl.pallas_call(
        hand_out,
        out_shape=tuple(jax.ShapeDtypeStruct(a.shape, a.dtype) for a in out),
        in_specs=[any_spec] * 5,
        out_specs=[any_spec] * 5,
        scratch_shapes=[pltpu.VMEM(a.shape, a.dtype) for a in out] + [dma((5,))] * 2,
        name="hand_out",
    )(*out)
    return (
        out[1].reshape(q_prompt.shape),
        out[0].reshape(q_resp.shape),
        out[2].reshape(kv_prompt.shape),
        out[3].reshape(kv_resp.shape),
        out[4],
    )


def solution(mesh):
    return jax.shard_map(
        shards,
        mesh=mesh,
        in_specs=(
            P("grp", "resp", "head", None),
            P("grp", "resp", None, "head", None),
            P("grp", None, "resp", "head", None),
            P("grp", "resp", None, None, "head", None),
            P("grp", "resp", "head", None),
            P("grp", "resp", None, "head", None),
            P(),
            P(),
            P("grp", "resp"),
            P("grp"),
        ),
        out_specs=(
            P("grp", "resp", "head", None),
            P("grp", "resp", None, "head", None),
            P("grp", None, "resp", "head", None),
            P("grp", "resp", None, None, "head", None),
            P(),
        ),
        check_vma=False,
    )
```

profile of v0, /device:TPU:1, one launch (start us, length us, event | category | flops | bytes accessed | tf_op | source)
XLA Modules:
  0.0 45.4 jit_solution(12920451758977011355)
XLA Ops:
  1.9 41.6 %attention_grads.1 = (bf16[1024,128]{1,0:T(8,128)(2,1)}, bf16[512,128]{1,0:T(8,128)(2,1)}, bf16[2,64,128]{2,1,0:T(8,128)(2,1)}, bf16[2,128,128]{2,1,0:T(8,128)(2,1)}, f32[2,128]{1,0:T(2,128)}) custom-call(bf16[1024,128]{1,0:T(8,128)(2,1)} %bitcast.16, bf16[512,128]{1,0:T(8,128)(2,1)} %bitcast.18, bf16[2,64,128]{2,1,0:T(8,128)(2,1)} %bitcast.21, ...), custom_call_target="tpu_custom_call" | custom-call | tf_op jit(solution)/shard_map/attention_grads/pallas_call | solution.py:520
  43.6 1.8 %hand_out.1 = (bf16[1024,128]{1,0:T(8,128)(2,1)}, bf16[512,128]{1,0:T(8,128)(2,1)}, bf16[2,64,128]{2,1,0:T(8,128)(2,1)}, bf16[2,128,128]{2,1,0:T(8,128)(2,1)}, f32[2,128]{1,0:T(2,128)}) custom-call(bf16[1024,128]{1,0:T(8,128)(2,1)} %get-tuple-element.15.refs_0_, bf16[512,128]{1,0:T(8,128)(2,1)} %get-tuple-element.16.refs_1_, ...), custom_call_target="tpu_custom_call" | custom-call | tf_op jit(solution)/shard_map/hand_out/pallas_call | solution.py:601
where the time goes:
time: 45.6 us; the launch traced here: 45.4 us
  Pallas kernels  43.5 us (95%)
  between operations  1.93 us (4%)
    pallas_call x1, Pallas kernels, shards(): pl.pallas_call(kernel, out_shape=(jax.ShapeDtypeStruct((rows_r, HD), BF),...  41.6 us
    pallas_call x1, Pallas kernels, shards(): pl.pallas_call(hand_out, out_shape=tuple((jax.ShapeDtypeStruct(a.shape, a...  1.81 us

commit v1 on v0

--- a/solution.py
+++ b/solution.py
@@ -196,6 +196,9 @@
         wait_for(kall.at[y_peer(dy)], kvy_got.at[(4 - dy) - 1])
         along_x(slot)
 
+    forward(1)
+    forward(2)
+
     for load in loads[6:]:
         load.wait()
     plen = plen_ref[0]
@@ -215,8 +218,6 @@
         qnt[:, sl] = qt
         qn[sl, :] = qt.T
 
-    forward(1)
-    forward(2)
     for k in range(7, 0, -1):
 
         @pl.when(grp >= k)
@@ -236,6 +237,8 @@
         else:
             keep = lane - rows_r < (plen - rows_p // 8 * resp) * 8
         dt[:, sl] = jnp.where(keep, d_nat[sl, :].T.astype(F32), 0.0)
+
+    forward(3)
 
     loads[3].wait()
     kf = kvr[0].astype(F32)
@@ -259,8 +262,6 @@
             ol[:, sl] = dot(vt1[:, pl.ds(0, nkr)], e)
         else:
             ol[:, sl] = jnp.zeros((HD + 16, TILE), F32)
-
-    forward(3)
 
     def pass1(step, carry):
         chunk = chunk_at(step)

time: 45.6 us -> 45.6 us (level)
  no operation moved by 1% of the time
where the time goes in v1:
time: 45.6 us; the launch traced here: 45.4 us
  Pallas kernels  43.5 us (95%)
  between operations  1.93 us (4%)
    pallas_call x1, Pallas kernels, shards(): pl.pallas_call(kernel, out_shape=(jax.ShapeDtypeStruct((rows_r, HD), BF),...  41.6 us
    pallas_call x1, Pallas kernels, shards(): pl.pallas_call(hand_out, out_shape=tuple((jax.ShapeDtypeStruct(a.shape, a...  1.81 us

profile of v1, /device:TPU:1, one launch (start us, length us, event | category | flops | bytes accessed | tf_op | source)
XLA Modules:
  0.0 45.4 jit_solution(8945509233619929128)
XLA Ops:
  1.9 41.6 %attention_grads.1 = (bf16[1024,128]{1,0:T(8,128)(2,1)}, bf16[512,128]{1,0:T(8,128)(2,1)}, bf16[2,64,128]{2,1,0:T(8,128)(2,1)}, bf16[2,128,128]{2,1,0:T(8,128)(2,1)}, f32[2,128]{1,0:T(2,128)}) custom-call(bf16[1024,128]{1,0:T(8,128)(2,1)} %bitcast.16, bf16[512,128]{1,0:T(8,128)(2,1)} %bitcast.18, bf16[2,64,128]{2,1,0:T(8,128)(2,1)} %bitcast.21, ...), custom_call_target="tpu_custom_call" | custom-call | tf_op jit(solution)/shard_map/attention_grads/pallas_call | solution.py:521
  43.6 1.8 %hand_out.1 = (bf16[1024,128]{1,0:T(8,128)(2,1)}, bf16[512,128]{1,0:T(8,128)(2,1)}, bf16[2,64,128]{2,1,0:T(8,128)(2,1)}, bf16[2,128,128]{2,1,0:T(8,128)(2,1)}, f32[2,128]{1,0:T(2,128)}) custom-call(bf16[1024,128]{1,0:T(8,128)(2,1)} %get-tuple-element.15.refs_0_, bf16[512,128]{1,0:T(8,128)(2,1)} %get-tuple-element.16.refs_1_, ...), custom_call_target="tpu_custom_call" | custom-call | tf_op jit(solution)/shard_map/hand_out/pallas_call | solution.py:602

commit v2 on v0

--- a/solution.py
+++ b/solution.py
@@ -417,10 +417,20 @@
             ).start()
         return carry
 
-    lax.fori_loop(0, NY, pass3, 0)
+    pass3(0, 0)
 
     g_finish(0)
     g_start(1)
+    pass3(1, 0)
+
+    g_finish(1)
+
+    @pl.when(grp < ngrp - 1)
+    def _():
+        pl.semaphore_wait(z_ready, ngrp - 1 - grp)
+
+    g_start(2)
+    lax.fori_loop(2, NY, pass3, 0)
 
     gvr = dot(er_ref[...], dst[:, pl.ds(0, rows_r)], NT)
     ur = ukr[...]
@@ -447,13 +457,6 @@
     stores[1].start()
     stores[2].start()
 
-    g_finish(1)
-
-    @pl.when(grp < ngrp - 1)
-    def _():
-        pl.semaphore_wait(z_ready, ngrp - 1 - grp)
-
-    g_start(2)
     for slot in (3, 2, 1):
         along_y(slot)
     wait_for(rx.at[0], rx_got.at[0])

time: 45.6 us -> 45.7 us (level)
  no operation moved by 1% of the time
where the time goes in v2:
time: 45.7 us; the launch traced here: 45.4 us
  Pallas kernels  43.5 us (95%)
  between operations  1.93 us (4%)
    pallas_call x1, Pallas kernels, shards(): pl.pallas_call(kernel, out_shape=(jax.ShapeDtypeStruct((rows_r, HD), BF),...  41.7 us
    pallas_call x1, Pallas kernels, shards(): pl.pallas_call(hand_out, out_shape=tuple((jax.ShapeDtypeStruct(a.shape, a...  1.81 us

profile of v2, /device:TPU:1, one launch (start us, length us, event | category | flops | bytes accessed | tf_op | source)
XLA Modules:
  0.0 45.4 jit_solution(13261644624559454687)
XLA Ops:
  1.9 41.7 %attention_grads.1 = (bf16[1024,128]{1,0:T(8,128)(2,1)}, bf16[512,128]{1,0:T(8,128)(2,1)}, bf16[2,64,128]{2,1,0:T(8,128)(2,1)}, bf16[2,128,128]{2,1,0:T(8,128)(2,1)}, f32[2,128]{1,0:T(2,128)}) custom-call(bf16[1024,128]{1,0:T(8,128)(2,1)} %bitcast.16, bf16[512,128]{1,0:T(8,128)(2,1)} %bitcast.18, bf16[2,64,128]{2,1,0:T(8,128)(2,1)} %bitcast.21, ...), custom_call_target="tpu_custom_call" | custom-call | tf_op jit(solution)/shard_map/attention_grads/pallas_call | solution.py:523
  43.6 1.8 %hand_out.1 = (bf16[1024,128]{1,0:T(8,128)(2,1)}, bf16[512,128]{1,0:T(8,128)(2,1)}, bf16[2,64,128]{2,1,0:T(8,128)(2,1)}, bf16[2,128,128]{2,1,0:T(8,128)(2,1)}, f32[2,128]{1,0:T(2,128)}) custom-call(bf16[1024,128]{1,0:T(8,128)(2,1)} %get-tuple-element.15.refs_0_, bf16[512,128]{1,0:T(8,128)(2,1)} %get-tuple-element.16.refs_1_, ...), custom_call_target="tpu_custom_call" | custom-call | tf_op jit(solution)/shard_map/hand_out/pallas_call | solution.py:604

commit v3 on v0

--- a/solution.py
+++ b/solution.py
@@ -344,7 +344,7 @@
         sums[step] = gk
         return carry
 
-    lax.fori_loop(0, NY, pass2, 0)
+    lax.fori_loop(0, NY, pass2, 0, unroll=2)
 
     gkr = jnp.zeros((nkr, HD), F32)
     for n in range(tiles_r):

time: 45.6 us -> 45.3 us (level)
  no operation moved by 1% of the time
where the time goes in v3:
time: 45.3 us; the launch traced here: 45.1 us
  Pallas kernels  43.1 us (95%)
  between operations  1.93 us (4%)
    pallas_call x1, Pallas kernels, shards(): pl.pallas_call(kernel, out_shape=(jax.ShapeDtypeStruct((rows_r, HD), BF),...  41.3 us
    pallas_call x1, Pallas kernels, shards(): pl.pallas_call(hand_out, out_shape=tuple((jax.ShapeDtypeStruct(a.shape, a...  1.81 us

profile of v3, /device:TPU:1, one launch (start us, length us, event | category | flops | bytes accessed | tf_op | source)
XLA Modules:
  0.0 45.1 jit_solution(17801056406066752723)
XLA Ops:
  1.9 41.3 %attention_grads.1 = (bf16[1024,128]{1,0:T(8,128)(2,1)}, bf16[512,128]{1,0:T(8,128)(2,1)}, bf16[2,64,128]{2,1,0:T(8,128)(2,1)}, bf16[2,128,128]{2,1,0:T(8,128)(2,1)}, f32[2,128]{1,0:T(2,128)}) custom-call(bf16[1024,128]{1,0:T(8,128)(2,1)} %bitcast.16, bf16[512,128]{1,0:T(8,128)(2,1)} %bitcast.18, bf16[2,64,128]{2,1,0:T(8,128)(2,1)} %bitcast.21, ...), custom_call_target="tpu_custom_call" | custom-call | tf_op jit(solution)/shard_map/attention_grads/pallas_call | solution.py:520
  43.3 1.8 %hand_out.1 = (bf16[1024,128]{1,0:T(8,128)(2,1)}, bf16[512,128]{1,0:T(8,128)(2,1)}, bf16[2,64,128]{2,1,0:T(8,128)(2,1)}, bf16[2,128,128]{2,1,0:T(8,128)(2,1)}, f32[2,128]{1,0:T(2,128)}) custom-call(bf16[1024,128]{1,0:T(8,128)(2,1)} %get-tuple-element.15.refs_0_, bf16[512,128]{1,0:T(8,128)(2,1)} %get-tuple-element.16.refs_1_, ...), custom_call_target="tpu_custom_call" | custom-call | tf_op jit(solution)/shard_map/hand_out/pallas_call | solution.py:601
